TPU v7x, 32 devices: a whole 2x2x4 slice. The times are simulated.
32 devices in a mesh: ch: 4 (over y, core), seq: 8 (over z, x).
Axes of the slice: x: 2, y: 2, z: 4, core: 2. Of those that a mesh axis runs over, the one named last changes fastest.
Arguments:
- tokens: bfloat16 [2, 4, 1024, 768], P(None, 'ch', 'seq'), may hold values from -6 to 6
- cotangent: bfloat16 [2, 4, 1024, 768], P(None, 'ch', 'seq'), may hold values from -6 to 6
- first_gain: bfloat16 [768], P(('ch', 'seq')), may hold values from 0.5 to 1.5
- first_shift: bfloat16 [768], P(('ch', 'seq')), may hold values from -1.1953125 to 1.1953125
- mixer_weight: bfloat16 [768, 2304], P(('ch', 'seq')), may hold values from -0.21875 to 0.21875
- mixer_bias: bfloat16 [2304], P(('ch', 'seq')), may hold values from -1.1953125 to 1.1953125
- short_weight: bfloat16 [3, 2304], P(None, ('ch', 'seq')), may hold values from -0.59765625 to 0.59765625
- short_bias: bfloat16 [2304], P(('ch', 'seq')), may hold values from -1.1953125 to 1.1953125
- embed_weight: float32 [33, 64], replicated, may hold values from -12 to 12
- embed_bias: float32 [64], replicated, may hold values from -3 to 3
- first_sine: float32 [64], replicated, may hold values from 0.5 to 1.5
- inner_weight: float32 [64, 64], replicated, may hold values from -12 to 12
- inner_bias: float32 [64], replicated, may hold values from -3 to 3
- second_sine: float32 [64], replicated, may hold values from 0.5 to 1.5
- filter_weight: float32 [64, 768], replicated, may hold values from -0.09375 to 0.09375
- decay_rate: float32 [768], replicated, may hold values from 0.00048828125 to 0.03
- long_bias: float32 [768], replicated, may hold values from -4 to 4
- output_weight: bfloat16 [768, 768], P(('ch', 'seq')), may hold values from -0.21875 to 0.21875
- output_bias: bfloat16 [768], P(('ch', 'seq')), may hold values from -1.1953125 to 1.1953125
- second_gain: bfloat16 [768], P(('ch', 'seq')), may hold values from 0.5 to 1.5
- second_shift: bfloat16 [768], P(('ch', 'seq')), may hold values from -1.1953125 to 1.1953125
- expand_weight: bfloat16 [768, 3072], P(('ch', 'seq')), may hold values from -0.21875 to 0.21875
- expand_bias: bfloat16 [3072], P(('ch', 'seq')), may hold values from -1.1953125 to 1.1953125
- shrink_weight: bfloat16 [3072, 768], P(('ch', 'seq')), may hold values from -0.15625 to 0.15625
- shrink_bias: bfloat16 [768], P(('ch', 'seq')), may hold values from -1.1953125 to 1.1953125
Outputs:
- block_out: bfloat16 [2, 4, 1024, 768], P(None, 'ch', 'seq')
- tokens_gradient: bfloat16 [2, 4, 1024, 768], P(None, 'ch', 'seq')
- first_gain_gradient: float32 [768], P(('ch', 'seq'))
- first_shift_gradient: float32 [768], P(('ch', 'seq'))
- mixer_weight_gradient: float32 [768, 2304], P(('ch', 'seq'))
- mixer_bias_gradient: float32 [2304], P(('ch', 'seq'))
- short_weight_gradient: float32 [3, 2304], P(None, ('ch', 'seq'))
- short_bias_gradient: float32 [2304], P(('ch', 'seq'))
- embed_weight_gradient: float32 [33, 64], replicated
- embed_bias_gradient: float32 [64], replicated
- first_sine_gradient: float32 [64], replicated
- inner_weight_gradient: float32 [64, 64], replicated
- inner_bias_gradient: float32 [64], replicated
- second_sine_gradient: float32 [64], replicated
- filter_weight_gradient: float32 [64, 768], replicated
- long_bias_gradient: float32 [768], replicated
- output_weight_gradient: float32 [768, 768], P(('ch', 'seq'))
- output_bias_gradient: float32 [768], P(('ch', 'seq'))
- second_gain_gradient: float32 [768], P(('ch', 'seq'))
- second_shift_gradient: float32 [768], P(('ch', 'seq'))
- expand_weight_gradient: float32 [768, 3072], P(('ch', 'seq'))
- expand_bias_gradient: float32 [3072], P(('ch', 'seq'))
- shrink_weight_gradient: float32 [3072, 768], P(('ch', 'seq'))
- shrink_bias_gradient: float32 [768], P(('ch', 'seq'))
All inputs are finite; a program needn't handle non-finite values.
Results may differ from a plain program's by a relative error of at most 0.013.
Values may be sent and summed in bfloat16 or wider, within the bound.
A program may use at most 320 MiB of HBM per device.

v0:
```python
import functools
import types

import jax
import jax.numpy as jnp
import numpy as np
from jax import lax
from jax.experimental import pallas as pl
from jax.experimental.pallas import tpu as pltpu
from jax.sharding import PartitionSpec as P


MESH = pl.DeviceIdType.MESH
f32 = jnp.float32
bf16 = jnp.bfloat16
LANES = 128
PIECES = ("mix", "out", "exp", "shr")


def dot_nn(left, right, precision=None):
    return lax.dot_general(
        left, right, (((1,), (0,)), ((), ())), precision=precision, preferred_element_type=f32
    )


def dot_nt(left, right, precision=None):
    return lax.dot_general(
        left, right, (((1,), (1,)), ((), ())), precision=precision, preferred_element_type=f32
    )


def dot_tn(left, right, precision=None):
    return lax.dot_general(
        left, right, (((0,), (0,)), ((), ())), precision=precision, preferred_element_type=f32
    )


def normalise(values):
    centre = values - jnp.mean(values, axis=-1, keepdims=True)
    scale = lax.rsqrt(jnp.mean(centre * centre, axis=-1, keepdims=True) + 1e-05)
    return centre * scale, scale


def norm_back(unit, scale, grad):
    inner = grad - jnp.mean(grad, axis=-1, keepdims=True)
    return scale * (inner - unit * jnp.mean(grad * unit, axis=-1, keepdims=True))


def sin_cos(angle):
    turns = jnp.floor(angle * (1.0 / np.pi) + 0.5)
    rest = angle - turns * 3.140625
    rest = rest - turns * 9.670257568359375e-4
    rest = rest - turns * 6.2771141529083251953e-7
    rest = rest - turns * 1.21644916362129151821e-10
    sign = 1.0 - 2.0 * (turns - 2.0 * jnp.floor(turns * 0.5))
    sq = rest * rest
    low = sq * (1.0 / 362880.0 - sq * (1.0 / 39916800.0 - sq * (1.0 / 6227020800.0)))
    sine = rest * (1.0 - sq * (1.0 / 6.0 - sq * (1.0 / 120.0 - sq * (1.0 / 5040.0 - low))))
    high = sq * (1.0 / 3628800.0 - sq * (1.0 / 479001600.0 - sq * (1.0 / 87178291200.0)))
    cosine = 1.0 - sq * (0.5 - sq * (1.0 / 24.0 - sq * (1.0 / 720.0 - sq * (1.0 / 40320.0 - high))))
    return sign * sine, sign * cosine


def split_two(value):
    top = value.astype(bf16)
    return top, (value - top.astype(f32)).astype(bf16)


def dot_two(dot, left, right):
    top, low = split_two(left)
    right = right.astype(bf16)
    return dot(top, right) + dot(low, right)


STEPS = {
    ("shrink",): (("s", 0),),
    ("expand",): (("s", 1), ("e", 0)),
    ("after", "grad"): (("t", 0),),
    ("conv_back", 0): (("s", 2),),
    ("conv_back", 1): (("o", 0), ("m0", 0)),
    ("conv_back", 2): (("e", 1),),
    ("before", "input"): (("e", 2), ("o", 1), ("m0", 1)),
    ("mixer", 1): (("m1", 0),),
    ("mixer", 2): (("m2", 0), ("o", 2), ("m0", 2), ("t", 1)),
    ("first", "norm"): (("m1", 1),),
    ("tokens",): (("m2", 1),),
    ("vectors",): (("t", 2), ("m1", 2), ("m2", 2)),
}


class Sizes:
    def __init__(self, chans, seqs, block, width, hidden):
        self.chans, self.seqs, self.block = chans, seqs, block
        self.width, self.hidden = width, hidden
        self.devices = chans * seqs
        self.y_n, self.z_n, self.x_n = chans // 2, seqs // 2, 2
        self.chips = self.devices // 2
        self.own = width // self.devices
        self.pair = 2 * self.own
        self.unit = hidden // self.devices
        self.cw = width // 2
        self.mw = 3 * self.cw
        self.hw = hidden // 2
        self.slab = 4 * self.own
        self.length = block * seqs
        self.tap = 3 * self.own
        self.blocks = {
            "mix": (self.pair, self.mw),
            "out": (self.pair, self.cw),
            "exp": (self.pair, self.hw),
            "shr": (self.unit, self.width),
        }
        third = self.cw // 3
        self.gathers = {
            "m": ("mix", self.cw, self.cw, self.cw),
            "g": ("mix", 0, 2 * third, third),
            "o": ("out", 0, third, 2 * third),
            "e": ("exp", 0, self.hw // 2, self.hw // 2),
            "s": ("shr", 0, 2 * third, 3 * third),
            "t": ("shr", 5 * third, third),
        }
        self.sums = {
            "s": ("shr", 0, 2 * third, 3 * third),
            "t": ("shr", 5 * third, third),
            "e": ("exp", 0, self.hw // 2, self.hw // 2),
            "o": ("out", 0, third, 2 * third),
            "m0": ("mix", 0, 2 * third, third),
            "m1": ("mix", self.cw, 2 * third, third),
            "m2": ("mix", 2 * self.cw, third, 2 * third),
        }


def tables(n):
    out = np.full((16, n.hw), -1, np.int32)
    p = np.arange(n.width)
    out[0, : n.width], out[1, : n.width] = p % n.own, p // n.own
    col = np.arange(n.mw)
    group, k = col // n.cw, col % n.cw
    chip, r = k // n.own, k % n.own
    for core in range(2):
        dev = (2 * (chip // n.seqs) + core) * n.seqs + chip % n.seqs
        e = group * n.width + n.own * dev + r
        out[2 + 2 * core, : n.mw], out[3 + 2 * core, : n.mw] = e % n.tap, e // n.tap
    col = np.arange(n.hw)
    chip, r = col // n.unit, col % n.unit
    out[6], out[7] = r, 2 * (chip // n.seqs) * n.seqs + chip % n.seqs
    chip, rest = p // n.pair, p % n.pair
    dev = (2 * (chip // n.seqs) + rest // n.own) * n.seqs + chip % n.seqs
    out[8, : n.width] = n.own * dev + rest % n.own
    return out


def encoding_table(length, bands, rows):
    positions = np.arange(length).astype(np.float32)
    frequency = np.linspace(0.0001, bands - 1, bands).astype(np.float32)
    angles = np.float32(2.0 * np.pi / length) * positions[:, None] * frequency[None, :]
    out = np.zeros((rows, length), np.float32)
    out[0] = positions / np.float32(length - 1)
    out[1 : 1 + bands] = np.cos(angles.astype(np.float64)).T
    out[1 + bands : 1 + 2 * bands] = -np.sin(angles.astype(np.float64)).T
    return out


INPUTS = (
    "tok", "cot", "i_gain1", "i_shift1", "i_mix", "i_mixb", "i_sw", "i_sb", "embw", "i_be", "i_fs", "inw", "i_bi",
    "i_ss", "i_filt", "i_rate", "i_skip", "i_out", "i_outb", "i_gain2", "i_shift2", "i_exp", "i_expb", "wshr",
    "i_shrb", "tabs", "enc",
)
OUTPUTS = ("bo", "tg", "gmix", "gexp", "gout", "gshr", "gsm", "fg", "gnet")
VECTORS = (
    "i_gain1", "i_shift1", "i_outb", "i_gain2", "i_shift2", "i_shrb", "i_mixb", None, None, None, "i_sb", "i_expb",
)


def scratch_list(n):
    v = pltpu.VMEM
    sem = pltpu.SemaphoreType.DMA
    rows = 4 * n.block
    half = 2 * n.block
    halo = 64
    slabs = (n.chips, n.slab, LANES)
    flat = (n.chips * n.slab, LANES)
    items = [
        ("xs", v((2, n.block, n.width), bf16)),
        ("gs", v((2, n.block, n.width), bf16)),
        ("ho", v((2, 16, n.width), bf16)),
        ("hs", v((2, 16, n.width), bf16)),
        ("pall", v((n.devices, 16, LANES), bf16)),
        ("pallf", v((n.devices * 16, LANES), f32)),
        ("wpre", v((n.pair, n.mw + n.hw), f32)),
        ("wrecv", v((n.own, n.mw + n.hw), f32)),
        ("pvf", v((16, LANES), f32)),
        ("pvec", v((16, LANES), bf16)),
        ("fvr", v((8, LANES), f32)),
        ("fvec", v((LANES, 8), f32)),
        ("fsel", v((n.own, LANES), f32)),
        ("pv", v((16, n.hw), f32)),
        ("r24", v((LANES, n.width), bf16)),
        ("r72", v((LANES, n.mw), bf16)),
        ("r96", v((LANES, n.hw), bf16)),
        ("d24", v((n.devices, n.width), f32)),
        ("d72", v((n.devices, n.mw), f32)),
        ("d96", v((n.devices, n.hw), f32)),
        ("perm", v((n.width, n.width), bf16)),
        ("n1p", v((rows + halo, n.width), bf16)),
        ("mixed", v((rows + halo, n.mw), bf16)),
        ("so", v((rows, n.mw), f32)),
        ("of", v(flat, f32)),
        ("gm", v(flat, f32)),
        ("uf", v(flat, f32)),
        ("gf", v(flat, f32)),
        ("toep", v((n.own, n.block, n.length), bf16)),
        ("u1", v((64, n.length), f32)),
        ("u2", v((64, n.length), f32)),
        ("l1", v((64, n.length), f32)),
        ("l2", v((LANES, n.length), f32)),
        ("c1", v((64, n.length), f32)),
        ("c2", v((64, n.length), f32)),
        ("imp", v((n.own, n.length), f32)),
        ("ig", v((n.own, n.length), f32)),
        ("w2o", v((n.cw, n.width), bf16)),
        ("low", v((rows, n.cw), bf16)),
        ("gated", v((rows, n.cw), bf16)),
        ("middle", v((rows, n.width), f32)),
        ("n2p", v((rows, n.width), bf16)),
        ("hid", v((rows, n.hw), bf16)),
        ("pre", v((rows, n.hw), bf16)),
        ("peo_s", v((rows, n.width), bf16)),
        ("peo_r", v((rows, n.width), bf16)),
        ("peb_s", v((half, n.width), bf16)),
        ("peb_r", v((half, n.width), bf16)),
        ("ped_r", v((rows, n.width), bf16)),
        ("pef_r", v((half, n.width), bf16)),
        ("acc", v((rows, n.width), f32)),
        ("branch", v((rows, n.width), bf16)),
        ("sg", v((rows, n.mw), f32)),
        ("nb_s", v((8, n.mw), f32)),
        ("nb_r", v((8, n.mw), f32)),
        ("mg", v((rows, n.mw), bf16)),
        ("msgs", v((n.devices * 16, LANES), f32)),
        ("rall", v((n.devices * 16, LANES), f32)),
        ("smf", v((8, LANES), f32)),
        ("msgf", v((n.devices * 8, LANES), f32)),
        ("rallf", v((n.devices * 8, LANES), f32)),
        ("fall", v((n.devices * 8, LANES), f32)),
        ("gv", v((16, n.hw), f32)),
    ]
    for k in range(4):
        items.append((f"sb{k}", v(slabs, bf16)))
        items.append((f"rb{k}", v(slabs, bf16)))
    for p in PIECES:
        r, c = n.blocks[p]
        items.append((f"w_{p}", v((n.chips, r, c), bf16)))
        if p != "exp":
            items.append((f"g_{p}", v((n.chips, r, c), bf16)))
        items.append((f"b_{p}", v((n.chips // 2, r, c), bf16)))
        items.append((f"a_{p}", v((n.chips // 4, r, c), bf16)))
        items.append((f"z_{p}", v((n.z_n - 1, r, c), bf16)))
    items += [
        ("ag_s", sem((2 * len(n.gathers),))),
        ("ag_r", sem((2 * len(n.gathers) * n.chips,))),
        ("rs_s", sem((6 * len(n.sums),))),
        ("rs_r", sem((6 * len(n.sums),))),
        ("ex_s", sem((28,))),
        ("ex_r", sem((28,))),
    ]
    return items


def fused_kernel(n, names, *refs):
    S = types.SimpleNamespace(**dict(zip(names, refs)))
    rows, half, blk = 4 * n.block, 2 * n.block, n.block
    S.tok_, S.cot_ = S.tok.at[:, 0], S.cot.at[:, 0]
    ch, seq = lax.axis_index("ch"), lax.axis_index("seq")
    y, core = lax.div(ch, 2), lax.rem(ch, 2)
    z, x = lax.div(seq, n.x_n), lax.rem(seq, n.x_n)
    me_dev = ch * n.seqs + seq
    other_ch = ch + 1 - 2 * core

    def chip(yy, zz, xx):
        return yy * n.seqs + zz * n.x_n + xx

    def slot(yy, zz, xx):
        return (zz * n.x_n + xx) * n.y_n + yy

    def at(yy, zz, xx):
        return (yy * 2 + core, zz * n.x_n + xx)

    me_chip, me_slot = chip(y, z, x), slot(y, z, x)
    sib = (other_ch, seq)

    def z_peer(j):
        peer = z
        bit = 1
        while bit <= j:
            if j & bit:
                peer = peer + bit * (1 - 2 * lax.rem(lax.div(z, bit), 2))
            bit *= 2
        return peer

    ends = []

    def send(src, dst, send_sem, recv_sem, target):
        pltpu.make_async_remote_copy(
            src_ref=src, dst_ref=dst, send_sem=send_sem, recv_sem=recv_sem,
            device_id=target, device_id_type=MESH,
        ).start()

    def wait(ref, sem):
        pltpu.make_async_copy(ref, ref, sem).wait()

    def later(ref, sem):
        ends.append((ref, sem))

    exchange_count = [0]

    def exchange(src, dst, target, free=False):
        k = exchange_count[0]
        exchange_count[0] += 1
        send(src, dst, S.ex_s.at[k], S.ex_r.at[k], target)
        if free:
            return lambda: wait(dst, S.ex_r.at[k]), lambda: wait(src, S.ex_s.at[k])
        later(src, S.ex_s.at[k])
        return lambda: wait(dst, S.ex_r.at[k])

    def to_others(src, dst, total):
        k = exchange_count[0]
        exchange_count[0] += 1
        for dc in range(n.chans):
            for ds in range(n.seqs):
                if dc or ds:
                    cc, ss = lax.rem(ch + dc, n.chans), lax.rem(seq + ds, n.seqs)
                    send(src(cc * n.seqs + ss), dst, S.ex_s.at[k], S.ex_r.at[k], (cc, ss))
        later(total, S.ex_s.at[k])
        return lambda: wait(total, S.ex_r.at[k])

    def to_chips(src, dst, total):
        k = exchange_count[0]
        exchange_count[0] += 1
        for dy in range(n.y_n):
            for dz in range(n.z_n):
                for dx in range(n.x_n):
                    if dy or dz or dx:
                        yy, zz, xx = lax.rem(y + dy, n.y_n), lax.rem(z + dz, n.z_n), lax.rem(x + dx, n.x_n)
                        send(src(yy, zz, xx), dst, S.ex_s.at[k], S.ex_r.at[k], at(yy, zz, xx))
        later(total, S.ex_s.at[k])
        return lambda: wait(total, S.ex_r.at[k])

    barrier = pltpu.get_barrier_semaphore()
    for dc in range(n.chans):
        for ds in range(n.seqs):
            if dc or ds:
                pl.semaphore_signal(
                    barrier, inc=1,
                    device_id=(lax.rem(ch + dc, n.chans), lax.rem(seq + ds, n.seqs)),
                    device_id_type=MESH,
                )
    theirs = pl.ds(pl.multiple_of((1 - core) * n.own, 8), n.own)
    ours = pl.ds(pl.multiple_of(core * n.own, 8), n.own)
    rows_mix, rows_exp = S.i_mix[...].astype(f32), S.i_exp[...].astype(f32)
    span, wide_span = n.cw // 2, n.hw // 2
    for k in range(2):
        to = slice(k * n.own, (k + 1) * n.own)
        for g in range(3):
            for yy in range(2):
                lo, src = g * n.cw + yy * span, g * n.width + (2 * yy + k) * span
                S.wpre[to, lo : lo + span] = rows_mix[:, src : src + span]
        for yy in range(2):
            lo, src = n.mw + yy * wide_span, (2 * yy + k) * wide_span
            S.wpre[to, lo : lo + wide_span] = rows_exp[:, src : src + wide_span]
    S.pvf[...] = jnp.zeros_like(S.pvf)
    for i, name in enumerate(VECTORS):
        if name:
            ref = getattr(S, name)
            size = ref.shape[0]
            S.pvf[i : i + 1, :size] = ref[...].astype(f32).reshape(1, size)
    S.pvf[7:10, : n.tap] = S.i_sw[...].astype(f32)
    S.pvec[...] = S.pvf[...].astype(bf16)
    S.w_shr[me_chip] = S.wshr[...]
    out_rows = S.i_out[...].astype(f32)
    S.w_out[me_chip] = jnp.concatenate([out_rows[:, : n.cw], out_rows[:, n.cw :]], axis=0).astype(bf16)

    def chosen(row, width):
        return S.tabs[row : row + 1, :width]

    def pick(row0, row1, width):
        return jnp.where(core == 0, chosen(row0, width), chosen(row1, width))

    def one_hot(height, index):
        return lax.broadcasted_iota(jnp.int32, (height, index.shape[1]), 0) == index

    S.r24[...] = one_hot(LANES, chosen(0, n.width)).astype(f32).astype(bf16)
    S.d24[...] = one_hot(n.devices, chosen(1, n.width)).astype(f32)
    S.r72[...] = one_hot(LANES, pick(2, 4, n.mw)).astype(f32).astype(bf16)
    S.d72[...] = one_hot(n.devices, pick(3, 5, n.mw)).astype(f32)

    pl.semaphore_wait(barrier, n.devices - 1)


    wait_pre, sent_pre = exchange(S.wpre.at[theirs], S.wrecv, sib, free=True)
    wait_xs = exchange(S.tok_, S.xs, sib)
    after = lax.rem(seq + 1, n.seqs)
    wait_ho = exchange(S.tok_.at[:, blk - 16 : blk, :], S.ho, (ch, after))
    wait_hs = exchange(S.tok_.at[:, blk - 16 : blk, :], S.hs, (other_ch, after))
    wait_params = to_others(
        lambda d: S.pvec, S.pall.at[me_dev], S.pall.at[pl.ds(0, n.devices - 1)]
    )
    wait_gs = exchange(S.cot_, S.gs, sib)
    S.pall[me_dev] = S.pvec[...]

    def flip(axis):
        return (1 - y, z, x) if axis == "y" else (y, z, 1 - x)

    far = (1 - y, z, 1 - x)

    class Line:
        def __init__(self, p, h):
            weight, start, *widths = n.gathers[p]
            self.buf = getattr(S, f"w_{weight}")
            self.cols = pl.ds(start + h * widths[0], widths[h])
            self.base = list(n.gathers).index(p) * 2 + h
            first, second = ("x", "y") if h == 0 else ("y", "x")
            self.first_dev, self.second_dev = at(*flip(first)), at(*flip(second))
            self.lead, self.side = flip(first), flip(second)

        def part(self, index):
            return self.buf.at[index, :, self.cols]

        def recv(self, k):
            return S.ag_r.at[self.base * n.chips + k]

        def push(self, index, k, target):
            send(self.part(index), self.part(index), S.ag_s.at[self.base], self.recv(k), target)

        def start_z(self):
            for j in range(1, n.z_n):
                self.push(me_chip, j, at(y, z_peer(j), x))

        def start_xy(self):
            self.push(me_chip, n.z_n, self.first_dev)
            self.push(me_chip, 2 * n.z_n, self.second_dev)

        def along(self, j):
            index = chip(y, z_peer(j), x)
            wait(self.part(index), self.recv(j))
            self.push(index, n.z_n + j, self.first_dev)
            self.push(index, 2 * n.z_n + j, self.second_dev)

        def across(self, j):
            index = chip(self.lead[0], z_peer(j), self.lead[2])
            wait(self.part(index), self.recv(n.z_n + j))
            self.push(index, 3 * n.z_n + j, self.second_dev)

        def finish(self):
            for j in range(n.z_n):
                wait(self.part(chip(self.side[0], z_peer(j), self.side[2])), self.recv(2 * n.z_n + j))
            for j in range(n.z_n):
                wait(self.part(chip(far[0], z_peer(j), far[2])), self.recv(3 * n.z_n + j))

        def sent(self):
            wait(self.buf.at[pl.ds(0, n.chips - 1), :, self.cols], S.ag_s.at[self.base])

    class Plane:
        def __init__(self, p):
            weight, start, width = n.gathers[p]
            self.buf = getattr(S, f"w_{weight}")
            self.cols = pl.ds(start, width)
            self.base = list(n.gathers).index(p) * 2
            self.x_dev, self.y_dev = at(*flip("x")), at(*flip("y"))
            self.x_chip, self.y_chip, self.far_chip = chip(*flip("x")), chip(*flip("y")), chip(*far)

        def part(self, index):
            return self.buf.at[index, :, self.cols]

        def recv(self, k):
            return S.ag_r.at[self.base * n.chips + k]

        def push(self, index, k, target):
            send(self.part(index), self.part(index), S.ag_s.at[self.base], self.recv(k), target)

        def start_xy(self):
            self.push(me_chip, 0, self.x_dev)
            self.push(me_chip, 1, self.y_dev)

        def corner(self):
            wait(self.part(self.x_chip), self.recv(0))
            self.push(self.x_chip, 2, self.y_dev)
            wait(self.part(self.y_chip), self.recv(1))

        def start_z(self):
            for j in range(1, n.z_n):
                self.push(me_chip, 3 + j, at(y, z_peer(j), x))
                self.push(self.x_chip, 2 + n.z_n + j, at(y, z_peer(j), x))
                self.push(self.y_chip, 1 + 2 * n.z_n + j, at(y, z_peer(j), x))

        def corner_z(self):
            wait(self.part(self.far_chip), self.recv(2))
            for j in range(1, n.z_n):
                self.push(self.far_chip, 3 * n.z_n + j, at(y, z_peer(j), x))

        def finish(self):
            for q, (yy, xx) in enumerate(((y, x), (y, 1 - x), (1 - y, x), (1 - y, 1 - x))):
                for j in range(1, n.z_n):
                    wait(self.part(chip(yy, z_peer(j), xx)), self.recv(3 - q + q * n.z_n + j))

        def sent(self):
            wait(self.part(pl.ds(0, n.chips - 1)), S.ag_s.at[self.base])

    gathers = {p: [Plane(p)] if p == "t" else [Line(p, 0), Line(p, 1)] for p in n.gathers}

    def gather(p, step, *args):
        for g in gathers[p]:
            getattr(g, step)(*args)

    gather("t", "start_xy")

    wait_pre()
    own_half, sib_half = S.wpre[ours, :], S.wrecv[...]
    slab = jnp.concatenate(
        [jnp.where(core == 0, own_half, sib_half), jnp.where(core == 0, sib_half, own_half)], axis=0
    ).astype(bf16)
    S.w_mix[me_chip] = slab[:, : n.mw]
    gather("m", "start_z")
    gather("m", "start_xy")
    S.w_exp[me_chip] = slab[:, n.mw :]

    todo = []

    def plan(p, step, *args):
        todo.extend(functools.partial(getattr(g, step), *args) for g in gathers[p])

    for p, then in (("m", "go"), ("go", "e"), ("e", "s"), ("s", "")):
        for j in range(1, n.z_n):
            for q in p:
                plan(q, "along", j)
        for q in then:
            plan(q, "start_z")
        if p == "m":
            plan("t", "corner")
        if p == "e":
            plan("t", "start_z")
            plan("t", "corner_z")
        for j in range(n.z_n):
            for q in p:
                plan(q, "across", j)
        for q in then:
            plan(q, "start_xy")
        if p == "m":
            mixer_steps = len(todo)
    plan_length = len(todo)

    def pump(count):
        for _ in range(min(count, len(todo))):
            todo.pop(0)()

    pump(2)
    S.perm[...] = one_hot(n.width, chosen(8, n.width)).astype(f32).astype(bf16)
    pump(2)
    wait_params()
    S.pallf[...] = S.pall[...].astype(f32).reshape(n.devices * 16, LANES)
    groups = [(range(0, 6), S.r24, S.d24), (range(6, 11), S.r72, S.d72), (range(11, 12), S.r96, S.d96)]

    def vectors_from_shards(members, right, mask):
        width = right.shape[1]
        for i in members:
            left = S.pallf[pl.ds(i, n.devices, stride=16), :].astype(bf16)
            S.pv[i : i + 1, :width] = jnp.sum(dot_nn(left, right[...]) * mask[...], axis=0, keepdims=True)

    vectors_from_shards(*groups[0])
    pump(2)

    def vector(i, lo=0, size=None):
        return S.pv[i : i + 1, lo : lo + (n.width if size is None else size)]

    hi = lax.Precision.HIGHEST

    def filter_setup():
        for i, ref in enumerate((S.i_be, S.i_fs, S.i_bi, S.i_ss)):
            S.fvr[i : i + 1, 0:64] = ref[...].reshape(1, 64)
        S.fvec[...] = jnp.transpose(S.fvr[...])
        last = [ref[...].reshape(1, n.width) for ref in (S.i_rate, S.i_skip)]
        last = jnp.concatenate(last + [jnp.zeros((6, n.width), f32)], axis=0)
        table = jnp.concatenate([S.i_filt[...], last], axis=0)
        first = lax.broadcasted_iota(jnp.int32, (n.own, n.width), 0) + me_dev * n.own
        mine = lax.broadcasted_iota(jnp.int32, (n.own, n.width), 1) == first
        S.fsel[:, : 72] = dot_nt(jnp.where(mine, 1.0, 0.0), table, hi)

    def filter_first():
        u = dot_tn(S.embw[...], S.enc[0 : S.embw.shape[0]], hi) + S.fvec[0:64, 0:1]
        S.u1[...] = u
        s, c = sin_cos(u * S.fvec[0:64, 1:2])
        S.l1[...] = s
        S.c1[...] = c

    def filter_second():
        u = dot_tn(S.inw[...], S.l1[...], hi) + S.fvec[0:64, 2:3]
        S.u2[...] = u
        s, c = sin_cos(u * S.fvec[0:64, 3:4])
        S.l2[0:64] = s
        row = lax.broadcasted_iota(jnp.int32, (LANES - 64, n.length), 0)
        col = lax.broadcasted_iota(jnp.int32, (LANES - 64, n.length), 1)
        S.l2[64:LANES] = jnp.where((row == 0) & (col == 0), 1.0, 0.0)
        S.c2[...] = c

    def decay():
        time = lax.broadcasted_iota(jnp.int32, (n.own, n.length), 1).astype(f32)
        return jnp.exp(-S.fsel[:, 64:65] * time)

    def filter_third():
        S.imp[...] = dot_nn(S.fsel[:, 0:64], S.l2[0:64], hi) * decay()

    def toeplitz(r):
        line = S.imp[pl.ds(r, 1), :]
        line = jnp.concatenate([jnp.zeros((1, LANES), f32), line], axis=1)
        wide = jnp.broadcast_to(line, (blk, LANES + n.length))
        S.toep[r] = pltpu.roll(wide, 0, 1, stride=1, stride_axis=0)[:, LANES:].astype(bf16)

    def norm_rows(values, gain, shift):
        unit, _ = normalise(values.astype(f32))
        low = (unit * vector(gain) + vector(shift)).astype(bf16)
        return dot_nn(low, S.perm[...]).astype(bf16)

    S.n1p[0:half] = norm_rows(S.tok_[...].reshape(half, n.width), 0, 1)
    pump(2)
    wait_xs()
    S.n1p[half:rows] = norm_rows(S.xs[...].reshape(half, n.width), 0, 1)
    pump(2)
    wait_ho()
    wait_hs()
    S.n1p[rows : rows + 32] = norm_rows(S.ho[...].reshape(32, n.width), 0, 1)
    S.n1p[rows + 32 : rows + 64] = norm_rows(S.hs[...].reshape(32, n.width), 0, 1)
    pump(4)

    pump(mixer_steps - (plan_length - len(todo)))
    vectors_from_shards(*groups[1])
    gather("m", "finish")
    pump(4)

    def project(g):
        lo = g * n.cw
        weight = S.w_mix[:, :, lo : lo + n.cw].reshape(n.width, n.cw)
        for r0, r1 in ((0, half), (half, rows + 64)):
            S.mixed[r0:r1, lo : lo + n.cw] = (
                dot_nn(S.n1p[r0:r1], weight) + vector(6, lo, n.cw)
            ).astype(bf16)
    first_block = seq == 0
    last_block = seq == n.seqs - 1

    def shifted(s, lo):
        own = S.mixed[s * blk : (s + 1) * blk, lo : lo + n.cw].astype(f32)
        before = S.mixed[rows + 16 * s : rows + 16 * (s + 1), lo : lo + n.cw].astype(f32)
        before = jnp.where(first_block, jnp.zeros_like(before), before)
        both = jnp.concatenate([before, own], axis=0)
        return own, pltpu.roll(both, 1, 0)[16:], pltpu.roll(both, 2, 0)[16:]

    def short_forward(g):
        lo = g * n.cw
        for s in range(4):
            now, one, two = shifted(s, lo)
            S.so[s * blk : (s + 1) * blk, lo : lo + n.cw] = (
                vector(7, lo, n.cw) * two + vector(8, lo, n.cw) * one
                + vector(9, lo, n.cw) * now + vector(10, lo, n.cw)
            )

    for g in (1, 2):
        project(g)
        short_forward(g)

    def token_rows(s):
        return slice(s * blk, (s + 1) * blk)

    def gate(s, g):
        return S.so[token_rows(s), g * n.cw : (g + 1) * n.cw]

    def to_channels(k, make):
        out, into = getattr(S, f"sb{k}"), getattr(S, f"rb{k}")
        for s in range(4):
            turned = jnp.transpose(make(s))
            for m in range(n.chips):
                row = m * n.slab + s * n.own
                S.of[row : row + n.own, :] = turned[m * n.own : (m + 1) * n.own]
        out[...] = S.of[...].astype(bf16).reshape(n.chips, n.slab, LANES)
        arrived = to_chips(
            lambda yy, zz, xx: out.at[chip(yy, zz, xx)], into.at[me_slot], into.at[pl.ds(0, n.chips - 1)]
        )
        into[me_slot] = out[me_chip]
        return arrived

    def to_tokens(k):
        out, into = getattr(S, f"sb{k}"), getattr(S, f"rb{k}")
        out[...] = S.of[...].astype(bf16).reshape(n.chips, n.slab, LANES)
        arrived = to_chips(
            lambda yy, zz, xx: out.at[slot(yy, zz, xx)], into.at[me_chip], into.at[pl.ds(0, n.chips - 1)]
        )
        into[me_chip] = out[me_slot]
        return arrived

    def token_view(k, s):
        got = getattr(S, f"rb{k}")[...].astype(f32)
        return jnp.transpose(got[:, s * n.own : (s + 1) * n.own, :].reshape(n.cw, LANES))

    wait_u = to_channels(0, lambda s: gate(s, 1) * gate(s, 2))
    third = n.own // 3
    pump(14)
    filter_setup()
    filter_first()
    filter_second()
    filter_third()
    S.r96[...] = one_hot(LANES, chosen(6, n.hw)).astype(f32).astype(bf16)
    S.d96[...] = one_hot(n.devices, chosen(7, n.hw) + core * n.seqs).astype(f32)
    vectors_from_shards(*groups[2])
    for q in range(3):
        lax.fori_loop(q * third, (q + 1) * third, lambda r, carry: (toeplitz(r), carry)[1], 0)
    pump(12)
    wait_u()

    group = n.y_n * 4
    lines = n.seqs * group
    S.uf[...] = S.rb0[...].astype(f32).reshape(n.chips * n.slab, LANES)

    def channel_rows(ref, r):
        return ref[pl.ds(r, lines, stride=n.own), :]

    def conv_forward(r, carry):
        own = channel_rows(S.uf, r)
        wide = dot_nn(own.astype(bf16), S.toep[r])
        blocks = []
        for i in range(n.seqs):
            total = wide[group * i : group * (i + 1), 0:LANES]
            for k in range(1, i + 1):
                total = total + wide[group * (i - k) : group * (i - k + 1), LANES * k : LANES * (k + 1)]
            blocks.append(total)
        result = jnp.concatenate(blocks, axis=0) + S.fsel[pl.ds(r, 1), 65:66] * own
        S.of[pl.ds(r, lines, stride=n.own), :] = result
        return carry

    for q in range(3):
        lax.fori_loop(q * third, (q + 1) * third, conv_forward, 0)
        pump(3)
    wait_low = to_tokens(1)
    pump(100)
    gather("g", "finish")
    project(0)
    short_forward(0)
    gather("o", "finish")
    slabs = S.w_out[...].astype(f32)
    S.w2o[:, : n.cw] = slabs[:, : n.own, :].reshape(n.cw, n.cw).astype(bf16)
    S.w2o[:, n.cw :] = slabs[:, n.own :, :].reshape(n.cw, n.cw).astype(bf16)
    wait_low()

    for s in range(4):
        low = token_view(1, s)
        S.low[token_rows(s)] = low.astype(bf16)
        S.gated[token_rows(s)] = (gate(s, 0) * low).astype(bf16)
    waits = []
    for part in (1, 0):
        r = slice(part * half, (part + 1) * half)
        o = slice((1 - part) * half, (2 - part) * half)
        S.acc[r] = dot_nn(S.gated[r], S.w2o[...])
        S.peo_s[r] = S.acc[r].astype(bf16)
        waits.append(exchange(S.peo_s.at[r], S.peo_r.at[o], sib, free=True))
    wait_gs()

    def tokens_of(part):
        return (S.tok_ if part == 0 else S.xs)[...].reshape(half, n.width).astype(f32)

    def cot_of(part):
        return (S.cot_ if part == 0 else S.gs)[...].reshape(half, n.width)

    for arrived, sent in waits:
        arrived()
        sent()
    for part in range(2):
        r = slice(part * half, (part + 1) * half)
        S.middle[r] = tokens_of(part) + (S.acc[r] + S.peo_r[r].astype(f32)) + vector(2)
        S.n2p[r] = norm_rows(S.middle[r], 3, 4)

    for p in "est":
        gather(p, "finish")
    chunk = n.hw // 4
    units = chunk // n.unit
    for q in range(4):
        lo = q * chunk
        weight = S.w_exp[:, :, lo : lo + chunk].reshape(n.width, chunk)
        shrink = S.w_shr[q * units : (q + 1) * units].reshape(chunk, n.width)
        total = jnp.zeros((1, chunk), f32)
        for part in range(2):
            r = slice(part * half, (part + 1) * half)
            v = dot_nn(S.n2p[r], weight) + vector(11, lo, chunk)
            back = dot_nt(cot_of(part), shrink)
            phi = 0.5 + 0.5 * lax.erf(v * np.float32(1.0 / np.sqrt(2.0)))
            slope = phi + v * (np.float32(1.0 / np.sqrt(2.0 * np.pi)) * jnp.exp(-0.5 * v * v))
            S.hid[r, lo : lo + chunk] = (v * phi).astype(bf16)
            pre = (back * slope).astype(bf16)
            S.pre[r, lo : lo + chunk] = pre
            total = total + jnp.sum(pre.astype(f32), axis=0, keepdims=True)
        S.gv[11:12, lo : lo + chunk] = total
    waits = []
    for part in (1, 0):
        r = slice(part * half, (part + 1) * half)
        o = slice((1 - part) * half, (2 - part) * half)
        S.acc[r] = dot_nt(S.pre[r], S.w_exp[...].reshape(n.width, n.hw))
        S.peo_s[r] = S.acc[r].astype(bf16)
        waits.append(exchange(S.peo_s.at[r], S.ped_r.at[o], sib))

    def gradient(weight):
        return S.w_exp if weight == "exp" else getattr(S, f"g_{weight}")

    def add_into(ref, index, cols, *terms):
        total = ref[index, :, cols].astype(f32)
        for term in terms:
            total = total + term.astype(f32)
        ref[index, :, cols] = total.astype(bf16)

    def scatter_line(p, h):
        weight, start, *widths = n.sums[p]
        grads, cols = gradient(weight), pl.ds(start + h * widths[0], widths[h])
        from_b, from_a, from_z = (getattr(S, f"{k}_{weight}") for k in "baz")
        base = list(n.sums).index(p) * 6 + h * 3
        second, first = ("y", "x") if h == 0 else ("x", "y")
        second_dev, first_dev = at(*flip(second)), at(*flip(first))

        def side(i):
            if second == "y":
                return y * n.seqs + i
            return chip(lax.div(i, n.z_n), lax.rem(i, n.z_n), x)

        def boxed(ref):
            return ref.reshape(n.y_n, n.z_n, n.x_n, *ref.shape[1:])

        def start_b():
            if second == "y":
                src, dst = grads.at[pl.ds((1 - y) * n.seqs, n.seqs), :, cols], from_b.at[:, :, cols]
            else:
                src = boxed(grads).at[:, :, 1 - x, :, cols]
                dst = from_b.reshape(n.y_n, n.z_n, *from_b.shape[1:]).at[:, :, :, cols]
            send(src, dst, S.rs_s.at[base], S.rs_r.at[base], second_dev)
            later(from_b.at[:, :, cols], S.rs_s.at[base])

        def end_b():
            wait(from_b.at[:, :, cols], S.rs_r.at[base])

            def add(i, carry):
                add_into(grads, side(i), cols, from_b[i, :, cols])
                return carry

            lax.fori_loop(0, n.chips // 2, add, 0)
            yy, xx = (y, 1 - x) if first == "x" else (1 - y, x)
            send(boxed(grads).at[yy, :, xx, :, cols], from_a.at[:, :, cols], S.rs_s.at[base + 1], S.rs_r.at[base + 1], first_dev)
            later(from_a.at[:, :, cols], S.rs_s.at[base + 1])

        def end_a():
            wait(from_a.at[:, :, cols], S.rs_r.at[base + 1])

            def add(zz, carry):
                add_into(grads, chip(y, zz, x), cols, from_a[zz, :, cols])
                return carry

            lax.fori_loop(0, n.z_n, add, 0)
            for j in range(1, n.z_n):
                send(
                    grads.at[chip(y, z_peer(j), x), :, cols], from_z.at[j - 1, :, cols],
                    S.rs_s.at[base + 2], S.rs_r.at[base + 2], at(y, z_peer(j), x),
                )
            later(from_z.at[:, :, cols], S.rs_s.at[base + 2])

        def end_z():
            wait(from_z.at[:, :, cols], S.rs_r.at[base + 2])
            total = grads[me_chip, :, cols].astype(f32)
            for j in range(n.z_n - 1):
                total = total + from_z[j, :, cols].astype(f32)
            return total

        return start_b, end_b, end_a, end_z

    def scatter_plane(p):
        weight, start, width = n.sums[p]
        grads, full = gradient(weight), pl.ds(start, width)
        eight, four, three = (getattr(S, f"{k}_{weight}") for k in "baz")
        base = list(n.sums).index(p) * 6
        plane = ((y, x), (y, 1 - x), (1 - y, x), (1 - y, 1 - x))
        x_dev, y_dev = at(*flip("x")), at(*flip("y"))
        x_chip, y_chip, far_chip = chip(*flip("x")), chip(*flip("y")), chip(*far)

        def landing(q, j):
            k = q * (n.z_n - 1) + j - 1
            many = n.chips // 2
            return (eight, k, 0) if k < many else (four, k - many, 1)

        def start_z():
            for q, (yy, xx) in enumerate(plane):
                for j in range(1, n.z_n):
                    ref, k, which = landing(q, j)
                    send(
                        grads.at[chip(yy, z_peer(j), xx), :, full], ref.at[k, :, full],
                        S.rs_s.at[base + which], S.rs_r.at[base + which], at(y, z_peer(j), x),
                    )
            later(eight.at[:, :, full], S.rs_s.at[base])
            later(four.at[:, :, full], S.rs_s.at[base + 1])

        def end_z():
            wait(eight.at[:, :, full], S.rs_r.at[base])
            wait(four.at[:, :, full], S.rs_r.at[base + 1])
            for q, (yy, xx) in enumerate(plane):
                terms = []
                for j in range(1, n.z_n):
                    ref, k, _ = landing(q, j)
                    terms.append(ref[k, :, full])
                add_into(grads, chip(yy, z, xx), full, *terms)
            send(grads.at[far_chip, :, full], three.at[0, :, full], S.rs_s.at[base + 2], S.rs_r.at[base + 2], x_dev)
            later(three.at[0, :, full], S.rs_s.at[base + 2])

        def end_corner():
            wait(three.at[0, :, full], S.rs_r.at[base + 2])
            add_into(grads, y_chip, full, three[0, :, full])
            for k, index, target in ((1, y_chip, y_dev), (2, x_chip, x_dev)):
                send(grads.at[index, :, full], three.at[k, :, full], S.rs_s.at[base + 3 + k], S.rs_r.at[base + 3 + k], target)
                later(three.at[k, :, full], S.rs_s.at[base + 3 + k])

        def end_xy():
            total = grads[me_chip, :, full].astype(f32)
            for k in (1, 2):
                wait(three.at[k, :, full], S.rs_r.at[base + 3 + k])
                total = total + three[k, :, full].astype(f32)
            return total

        return start_z, end_z, end_corner, end_xy

    scatters = {p: [scatter_plane(p)] if p == "t" else [scatter_line(p, h) for h in range(2)] for p in n.sums}

    def scatter(p, stage):
        return [s[stage]() for s in scatters[p]]

    def steps(*place):
        for p, stage in STEPS.get(place, ()):
            scatter(p, stage)

    all_cot = jnp.concatenate([cot_of(0), cot_of(1)], axis=0)
    for q in range(4):
        lo = q * chunk
        S.g_shr[q * units : (q + 1) * units] = (
            dot_tn(S.hid[:, lo : lo + chunk], all_cot).astype(bf16).reshape(units, n.unit, n.width)
        )
    steps("shrink")
    S.gv[5:6, : n.width] = jnp.sum(cot_of(0).astype(f32), axis=0, keepdims=True)
    for w in waits:
        w()

    for part in range(2):
        r = slice(part * half, (part + 1) * half)
        grad = dot_nt((S.acc[r] + S.ped_r[r].astype(f32)).astype(bf16), S.perm[...])
        unit, scale = normalise(S.middle[r])
        if part == 0:
            S.gv[3:4, : n.width] = jnp.sum(grad * unit, axis=0, keepdims=True)
            S.gv[4:5, : n.width] = jnp.sum(grad, axis=0, keepdims=True)
        total = cot_of(part).astype(f32) + norm_back(unit, scale, grad * vector(3))
        S.acc[r] = total
        S.branch[r] = total.astype(bf16)

    for s in range(4):
        S.sg[token_rows(s), : n.cw] = dot_nt(S.branch[token_rows(s)], S.w2o[...])
    wait_g = to_channels(2, lambda s: S.sg[token_rows(s), : n.cw] * gate(s, 0))
    for s in range(4):
        S.sg[token_rows(s), : n.cw] = S.sg[token_rows(s), : n.cw] * S.low[token_rows(s)].astype(f32)

    def send_heads(lo, width):
        head_row = lax.broadcasted_iota(jnp.int32, (8, width), 0)
        heads = jnp.zeros((8, width), f32)
        for s in range(4):
            top = S.sg[s * blk : s * blk + 8, lo : lo + width]
            heads = heads + jnp.where(lax.div(head_row, 2) == s, pltpu.roll(top, 2 * s, 0) if s else top, 0.0)
        cols = pl.ds(lo, width)
        S.nb_s[:, cols] = heads
        return exchange(S.nb_s.at[:, cols], S.nb_r.at[:, cols], (ch, lax.rem(seq + n.seqs - 1, n.seqs)))

    def tap_sums(g):
        lo = g * n.cw
        sums = [jnp.zeros((1, n.cw), f32) for _ in range(4)]
        for s in range(4):
            grad = S.sg[token_rows(s), lo : lo + n.cw]
            now, one, two = shifted(s, lo)
            for i, term in enumerate((grad * two, grad * one, grad * now, grad)):
                sums[i] = sums[i] + jnp.sum(term, axis=0, keepdims=True)
        for i in range(4):
            S.gv[7 + i : 8 + i, lo : lo + n.cw] = sums[i]

    def mixed_back(g):
        lo = g * n.cw
        total = jnp.zeros((1, n.cw), f32)
        nexts = S.nb_r[:, lo : lo + n.cw]
        nexts = jnp.where(last_block, jnp.zeros_like(nexts), nexts)
        for s in range(4):
            grad = S.sg[token_rows(s), lo : lo + n.cw]
            tail = pltpu.roll(nexts, 8 - 2 * s, 0) if s else nexts
            both = jnp.concatenate([grad, tail], axis=0)
            low = (
                vector(9, lo, n.cw) * grad
                + vector(8, lo, n.cw) * pltpu.roll(both, blk + 7, 0)[:blk]
                + vector(7, lo, n.cw) * pltpu.roll(both, blk + 6, 0)[:blk]
            ).astype(bf16)
            S.mg[token_rows(s), lo : lo + n.cw] = low
            total = total + jnp.sum(low.astype(f32), axis=0, keepdims=True)
        S.gv[6:7, lo : lo + n.cw] = total
        S.g_mix[:, :, lo : lo + n.cw] = (
            dot_tn(S.n1p[0:rows], S.mg[:, lo : lo + n.cw]).astype(bf16).reshape(n.chips, n.pair, n.cw)
        )

    S.msgs[...] = jnp.zeros_like(S.msgs)

    def pack(members, right, mask):
        width = right.shape[1]
        value = jnp.concatenate([S.gv[i : i + 1, :width] * mask[...] for i in members], axis=0)
        shards = dot_two(dot_nt, value, right[...])
        for k, i in enumerate(members):
            S.msgs[pl.ds(i, n.devices, stride=16), :] = shards[k * n.devices : (k + 1) * n.devices]

    wait_nb = send_heads(0, n.cw)
    steps("heads")
    S.gv[2:3, : n.width] = jnp.sum(S.branch[0:half].astype(f32), axis=0, keepdims=True)
    gather("e", "sent")
    for q in range(4):
        lo = q * chunk
        S.w_exp[:, :, lo : lo + chunk] = (
            dot_tn(S.n2p[...], S.pre[:, lo : lo + chunk]).astype(bf16).reshape(n.chips, n.pair, chunk)
        )

    steps("expand")

    for part in (1, 0):
        r = slice(part * half, (part + 1) * half)
        value = dot_nn(S.hid[r], S.w_shr[...].reshape(n.hw, n.width))
        if part:
            S.peb_s[...] = value.astype(bf16)
            wait_bo, sent_bo = exchange(S.peb_s, S.peb_r, sib, free=True)
        else:
            S.middle[r] = S.middle[r] + value + vector(5)
    outs = dot_tn(S.gated[...], S.branch[...]).reshape(n.chips, n.own, n.width)
    S.g_out[...] = jnp.concatenate([outs[:, :, : n.cw], outs[:, :, n.cw :]], axis=1).astype(bf16)
    steps("output")
    tap_sums(0)
    wait_nb()
    mixed_back(0)
    steps("mixer", 0)
    pack((2, 3, 4, 5), S.r24, S.d24)
    pack((11,), S.r96, S.d96)
    wait_bo()
    sent_bo()
    S.bo[...] = (S.middle[0:half] + S.peb_r[...].astype(f32)).astype(bf16).reshape(2, blk, n.width)
    steps("before", "grad")
    wait_g()
    steps("after", "grad")

    flat = lax.broadcasted_iota(jnp.int32, (blk, blk), 0) + lax.broadcasted_iota(jnp.int32, (blk, blk), 1)
    mirror = jnp.where(flat == blk - 1, 1.0, 0.0).astype(bf16)
    S.gf[...] = S.rb2[...].astype(f32).reshape(n.chips * n.slab, LANES)
    S.gm[...] = dot_nn(S.rb2[...].reshape(n.chips * n.slab, LANES), mirror)
    S.uf[...] = dot_nn(S.rb0[...].reshape(n.chips * n.slab, LANES), mirror)

    def conv_back(r, carry):
        turned = channel_rows(S.gm, r)
        wide = dot_nn(turned.astype(bf16), S.toep[r])
        blocks = []
        for i in range(n.seqs):
            total = wide[group * i : group * (i + 1), 0:LANES]
            for k in range(1, n.seqs - i):
                total = total + wide[group * (i + k) : group * (i + k + 1), LANES * k : LANES * (k + 1)]
            blocks.append(total)
        back = jnp.concatenate(blocks, axis=0) + S.fsel[pl.ds(r, 1), 65:66] * turned
        S.of[pl.ds(r, lines, stride=n.own), :] = dot_nn(back.astype(bf16), mirror)
        grad = channel_rows(S.gf, r)
        steps = [grad]
        for k in range(1, n.seqs):
            steps.append(
                jnp.concatenate([grad[group * k :], jnp.zeros((group * k, LANES), f32)], axis=0)
            )
        ahead = jnp.concatenate(steps, axis=1).astype(bf16)
        outer = dot_tn(channel_rows(S.uf, r).astype(bf16), ahead)
        outer = jnp.concatenate([jnp.zeros((blk, LANES), f32), outer], axis=1)
        outer = pltpu.roll(outer, n.length + 1, 1, stride=1, stride_axis=0)
        S.ig[pl.ds(r, 1), :] = jnp.sum(outer, axis=0, keepdims=True)[:, LANES:]
        return carry

    for q in range(3):
        lax.fori_loop(q * third, (q + 1) * third, conv_back, 0)
        if q == 2:
            wait_in = to_tokens(3)
        steps("conv_back", q)

    d_line = S.ig[...] * decay()
    fg_rows = pl.ds(pl.multiple_of(me_dev * n.own, 8), n.own)
    S.fg[fg_rows, :] = dot_two(dot_nt, d_line, S.l2[...])
    wait_fg = to_chips(lambda yy, zz, xx: S.fg.at[fg_rows], S.fg.at[fg_rows], S.fg.at[pl.ds(0, (n.chips - 1) * n.own)])
    steps("filter")
    top, low = split_two(d_line)
    wide_filter = S.fsel[:, 0:64].astype(bf16)
    d_l2 = (dot_tn(wide_filter, top) + dot_tn(wide_filter, low)) * S.c2[...]
    d_u2 = d_l2 * S.fvec[0:64, 3:4]
    top, low = split_two(d_u2)
    inner = S.inw[...].astype(bf16)
    d_l1 = (dot_nn(inner, top) + dot_nn(inner, low)) * S.c1[...]
    d_u1 = d_l1 * S.fvec[0:64, 1:2]
    l1, enc = S.l1[...].astype(bf16), S.enc[...].astype(bf16)
    net = jnp.concatenate([dot_nt(top, l1) + dot_nt(low, l1), dot_two(dot_nt, d_u1, enc)], axis=1)
    net_lane = lax.broadcasted_iota(jnp.int32, (64, LANES), 1)
    for i, term in enumerate((d_u1, d_l1 * S.u1[...], d_u2, d_l2 * S.u2[...])):
        net = jnp.where(net_lane == LANES - 8 + i, jnp.sum(term, axis=1, keepdims=True), net)
    S.msgf[...] = jnp.zeros_like(S.msgf)
    S.msgf[pl.ds(0, n.devices, stride=8), :] = net[0 : n.devices]
    S.msgf[pl.ds(1, n.devices, stride=8), :] = net[n.devices :]

    def eight(d):
        return pl.ds(pl.multiple_of(d * 8, 8), 8)

    wait_msgf = to_others(
        lambda d: S.msgf.at[eight(d)], S.rallf.at[eight(me_dev)], S.rallf.at[pl.ds(0, (n.devices - 1) * 8)]
    )
    S.rallf[eight(me_dev), :] = S.msgf[eight(me_dev), :]
    steps("before", "input")
    wait_in()

    for s in range(4):
        grad = token_view(3, s)
        S.sg[token_rows(s), n.cw : 2 * n.cw] = grad * gate(s, 2)
        S.sg[token_rows(s), 2 * n.cw :] = grad * gate(s, 1)
    wait_nb = send_heads(n.cw, 2 * n.cw)
    wait_msgf()
    S.smf[...] = jnp.sum(S.rallf[...].reshape(n.devices, 8, LANES), axis=0)
    wait_net = to_others(lambda d: S.smf, S.fall.at[eight(me_dev)], S.fall.at[pl.ds(0, (n.devices - 1) * 8)])
    S.fall[eight(me_dev), :] = S.smf[...]
    wait_fg()
    sib_waits = []
    for yy in range(n.y_n):
        span = pl.ds(pl.multiple_of((yy * 2 + core) * n.seqs * n.own, 8), n.seqs * n.own)
        sib_span = pl.ds(pl.multiple_of((yy * 2 + 1 - core) * n.seqs * n.own, 8), n.seqs * n.own)
        k = exchange_count[0]
        exchange_count[0] += 1
        send(S.fg.at[span], S.fg.at[span], S.ex_s.at[k], S.ex_r.at[k], sib)
        later(S.fg.at[span], S.ex_s.at[k])
        sib_waits.append((sib_span, k))
    steps("next", "heads")
    tap_sums(1)
    tap_sums(2)
    wait_nb()
    mixed_back(1)
    steps("mixer", 1)
    mixed_back(2)
    steps("mixer", 2)
    weight = S.w_mix[...].reshape(n.width, n.mw)
    S.peb_s[...] = dot_nt(S.mg[half:rows], weight).astype(bf16)
    wait_f = exchange(S.peb_s, S.pef_r, sib)
    pack(range(6, 11), S.r72, S.d72)
    mine = dot_nt(S.mg[0:half], weight)
    steps("first", "norm")
    wait_f()
    grad = dot_nt((mine + S.pef_r[...].astype(f32)).astype(bf16), S.perm[...])
    unit, scale = normalise(tokens_of(0))
    S.gv[0:1, : n.width] = jnp.sum(grad * unit, axis=0, keepdims=True)
    S.gv[1:2, : n.width] = jnp.sum(grad, axis=0, keepdims=True)
    S.tg[...] = (S.acc[0:half] + norm_back(unit, scale, grad * vector(0))).astype(bf16).reshape(2, blk, n.width)

    steps("tokens")

    pack((0, 1), S.r24, S.d24)

    def message(d):
        return pl.ds(pl.multiple_of(d * 16, 16), 16)

    wait_msgs = to_others(
        lambda d: S.msgs.at[message(d)], S.rall.at[message(me_dev)], S.rall.at[pl.ds(0, (n.devices - 1) * 16)]
    )
    S.rall[message(me_dev), :] = S.msgs[message(me_dev), :]
    steps("vectors")

    wait_msgs()
    S.gsm[...] = jnp.sum(S.rall[...].reshape(n.devices, 16, LANES), axis=0)
    sent_pre()

    def finish(p, ref, at_col):
        lo = at_col
        for value in scatter(p, 3):
            ref[:, lo : lo + value.shape[1]] = value
            lo += value.shape[1]

    finish("s", S.gshr, 0)
    finish("t", S.gshr, n.sums["t"][1])
    both = jnp.concatenate(scatter("o", 3), axis=1)
    S.gout[:, : n.cw], S.gout[:, n.cw :] = both[: n.own], both[n.own :]
    finish("e", S.wpre, n.mw)
    finish("m0", S.wpre, 0)
    for span, k in sib_waits:
        wait(S.fg.at[span], S.ex_r.at[k])
    finish("m1", S.wpre, n.cw)
    finish("m2", S.wpre, 2 * n.cw)
    wait_fin = exchange(S.wpre.at[theirs], S.wrecv, sib)
    S.gmix[core] = S.wpre[ours, : n.mw]
    S.gexp[core] = S.wpre[ours, n.mw :]
    wait_net()
    S.gnet[0 : n.devices] = S.fall[pl.ds(0, n.devices, stride=8), :]
    S.gnet[n.devices :] = S.fall[pl.ds(1, n.devices, stride=8), :]
    wait_fin()
    S.gmix[1 - core] = S.wrecv[:, : n.mw]
    S.gexp[1 - core] = S.wrecv[:, n.mw :]
    for p in "mgost":
        gather(p, "sent")
    for ref, sem in ends:
        wait(ref, sem)


def emit_kernel(n, emb, bo, tg, gmix, gexp, gout, gshr, gsm, fg, gnet, *outs):
    (o_bo, o_tg, o_g1, o_s1, o_mix, o_mixb, o_sw, o_sb, o_embw, o_be, o_fs, o_inw, o_bi, o_ss, o_fw, o_lb, o_out,
     o_outb, o_g2, o_s2, o_exp, o_expb, o_shr, o_shrb) = outs
    o_bo[:, 0], o_tg[:, 0] = bo[...], tg[...]
    span, wide_span = n.cw // 2, n.hw // 2
    for k in range(2):
        for yy in range(2):
            for g in range(3):
                lo, dst = g * n.cw + yy * span, g * n.width + (2 * yy + k) * span
                o_mix[:, dst : dst + span] = gmix[k, :, lo : lo + span]
            lo, dst = yy * wide_span, (2 * yy + k) * wide_span
            o_exp[:, dst : dst + wide_span] = gexp[k, :, lo : lo + wide_span]
    o_out[...], o_shr[...] = gout[...], gshr[...]
    for i, ref in ((0, o_g1), (1, o_s1), (2, o_outb), (3, o_g2), (4, o_s2), (5, o_shrb), (6, o_mixb), (10, o_sb), (11, o_expb)):
        size = ref.shape[0]
        ref[...] = gsm[i : i + 1, :size].reshape(size)
    o_sw[...] = gsm[7:10, : n.tap]
    net = jnp.transpose(gnet[...])
    o_inw[...] = net[0:64]
    o_embw[...] = net[64 : 64 + emb]
    for i, ref in enumerate((o_be, o_fs, o_bi, o_ss)):
        ref[...] = net[LANES - 8 + i : LANES - 7 + i].reshape(64)
    filt = jnp.transpose(fg[...])
    o_fw[...] = filt[0:64]
    o_lb[...] = filt[64:65].reshape(n.width)


def fused(n, *args):
    emb = args[8].shape[0]
    tables_in = (jnp.asarray(tables(n)), jnp.asarray(encoding_table(n.length, (emb - 1) // 2, 64)))
    shape = jax.ShapeDtypeStruct
    outs = (
        shape((2, n.block, n.width), bf16), shape((2, n.block, n.width), bf16),
        shape((2, n.own, n.mw), f32), shape((2, n.own, n.hw), f32), shape((n.own, n.width), f32),
        shape((n.unit, n.width), f32), shape((16, LANES), f32), shape((n.width, LANES), f32),
        shape((64, LANES), f32),
    )
    scratch = scratch_list(n)
    names = INPUTS + OUTPUTS + tuple(name for name, _ in scratch)
    vmem = pl.BlockSpec(memory_space=pltpu.VMEM)
    results = pl.pallas_call(
        functools.partial(fused_kernel, n, names),
        out_shape=outs,
        in_specs=[vmem] * len(INPUTS),
        out_specs=[vmem] * len(outs),
        scratch_shapes=[s for _, s in scratch],
        compiler_params=pltpu.CompilerParams(
            collective_id=0, has_side_effects=True, vmem_limit_bytes=63 << 20
        ),
    )(*args, *tables_in)
    like = args[:1] * 2 + args[2:15] + args[16:]
    final = tuple(shape(a.shape, f32 if i > 1 else bf16) for i, a in enumerate(like))
    return pl.pallas_call(
        functools.partial(emit_kernel, n, emb),
        out_shape=final,
        in_specs=[vmem] * len(outs),
        out_specs=[vmem] * len(final),
        compiler_params=pltpu.CompilerParams(vmem_limit_bytes=63 << 20),
    )(*results)


highest = lax.Precision.HIGHEST


def from_behind(block, axis, distance):
    devices = range(lax.axis_size(axis))
    route = [(i - distance, i) for i in devices if i - distance in devices]
    return lax.ppermute(block, axis, route)


def matmul(left, right):
    return jnp.dot(left, right, precision=highest, preferred_element_type=jnp.float32)


def layer_norm(values, gain, shift):
    centre = values - jnp.mean(values, axis=-1, keepdims=True)
    spread = jnp.mean(centre * centre, axis=-1, keepdims=True)
    return centre * lax.rsqrt(spread + 1e-05) * gain + shift


def exact_gelu(values):
    return jax.nn.gelu(values, approximate=False)


def filter_values(
    seq_length,
    embed_matrix,
    embed_offset,
    sine_first,
    inner_matrix,
    inner_offset,
    sine_second,
    head_matrix,
    rates,
):
    positions = jnp.arange(seq_length).astype(jnp.float32)
    band_count = (embed_matrix.shape[0] - 1) // 2
    frequency = jnp.linspace(0.0001, band_count - 1, band_count).astype(jnp.float32)
    angles = 2.0 * jnp.pi / seq_length * positions[:, None] * frequency[None, :]
    encoded = jnp.concatenate(
        [positions[:, None] / (seq_length - 1), jnp.cos(angles), -jnp.sin(angles)], axis=1
    )
    layer_first = jnp.sin(sine_first * (matmul(encoded, embed_matrix) + embed_offset))
    layer_second = jnp.sin(sine_second * (matmul(layer_first, inner_matrix) + inner_offset))
    return matmul(layer_second, head_matrix) * jnp.exp(-rates[None, :] * positions[:, None])


def spectral_tables(block_rows):
    period = 2 * block_rows
    freq_rows = jnp.arange(block_rows + 1)
    sample_cols = jnp.arange(period)
    phase = (freq_rows[:, None] * sample_cols[None, :] % period).astype(jnp.float32) * (
        2.0 * jnp.pi / period
    )
    forward_full = jnp.concatenate([jnp.cos(phase), -jnp.sin(phase)], axis=0)
    out_times = jnp.arange(block_rows) + block_rows
    out_phase = (out_times[:, None] * freq_rows[None, :] % period).astype(jnp.float32) * (
        2.0 * jnp.pi / period
    )
    edge = (freq_rows == 0) | (freq_rows == block_rows)
    factor = jnp.where(edge, 1.0, 2.0).astype(jnp.float32) / period
    inverse_table = jnp.concatenate(
        [factor[None, :] * jnp.cos(out_phase), -factor[None, :] * jnp.sin(out_phase)], axis=1
    )
    return (forward_full, inverse_table)


def spec_product(filt, spectrum):
    return jnp.stack(
        [
            filt[0] * spectrum[0] - filt[1] * spectrum[1],
            filt[0] * spectrum[1] + filt[1] * spectrum[0],
        ]
    )


def spec_adjoint(filt, grad_spec):
    return jnp.stack(
        [
            filt[0] * grad_spec[0] + filt[1] * grad_spec[1],
            filt[0] * grad_spec[1] - filt[1] * grad_spec[0],
        ]
    )


def contract_rows(left, right):
    return lax.dot_general(
        left, right, (((0,), (0,)), ((), ())), preferred_element_type=jnp.float32
    )


def contract_cols(left, right):
    return lax.dot_general(
        left, right, (((1,), (1,)), ((), ())), preferred_element_type=jnp.float32
    )


def on_device(
    tokens,
    cotangent,
    first_gain,
    first_shift,
    mixer_weight,
    mixer_bias,
    short_weight,
    short_bias,
    embed_weight,
    embed_bias,
    first_sine,
    inner_weight,
    inner_bias,
    second_sine,
    filter_weight,
    decay_rate,
    long_bias,
    output_weight,
    output_bias,
    second_gain,
    second_shift,
    expand_weight,
    expand_bias,
    shrink_weight,
    shrink_bias,
):
    chan_count = lax.axis_size("ch")
    seq_count = lax.axis_size("seq")
    chan_index = lax.axis_index("ch")
    seq_index = lax.axis_index("seq")
    block_rows = tokens.shape[2]
    width = tokens.shape[3]
    span_width = width // chan_count
    seq_length = block_rows * seq_count
    freq_count = block_rows + 1
    gathered = (
        lax.all_gather(first_gain, ("ch", "seq"), axis=0, tiled=True),
        lax.all_gather(first_shift, ("ch", "seq"), axis=0, tiled=True),
        lax.all_gather(mixer_weight, ("ch", "seq"), axis=0, tiled=True),
        lax.all_gather(mixer_bias, ("ch", "seq"), axis=0, tiled=True),
        lax.all_gather(short_weight, ("ch", "seq"), axis=1, tiled=True),
        lax.all_gather(short_bias, ("ch", "seq"), axis=0, tiled=True),
        lax.all_gather(output_weight, ("ch", "seq"), axis=0, tiled=True),
        lax.all_gather(output_bias, ("ch", "seq"), axis=0, tiled=True),
        lax.all_gather(second_gain, ("ch", "seq"), axis=0, tiled=True),
        lax.all_gather(second_shift, ("ch", "seq"), axis=0, tiled=True),
        lax.all_gather(expand_weight, ("ch", "seq"), axis=0, tiled=True),
        lax.all_gather(expand_bias, ("ch", "seq"), axis=0, tiled=True),
        lax.all_gather(shrink_weight, ("ch", "seq"), axis=0, tiled=True),
        lax.all_gather(shrink_bias, ("ch", "seq"), axis=0, tiled=True),
    )
    (
        gain_one,
        shift_one,
        mix_matrix,
        mix_offset,
        short_taps,
        short_offset,
        out_matrix,
        out_offset,
        gain_two,
        shift_two,
        expand_matrix,
        expand_offset,
        shrink_matrix,
        shrink_offset,
    ) = gathered
    gain_one_f = gain_one.astype(jnp.float32)
    shift_one_f = shift_one.astype(jnp.float32)
    mix_offset_f = mix_offset.astype(jnp.float32)
    taps_f = short_taps.astype(jnp.float32)
    short_offset_f = short_offset.astype(jnp.float32)
    out_offset_f = out_offset.astype(jnp.float32)
    gain_two_f = gain_two.astype(jnp.float32)
    shift_two_f = shift_two.astype(jnp.float32)
    expand_offset_f = expand_offset.astype(jnp.float32)
    shrink_offset_f = shrink_offset.astype(jnp.float32)

    def local_filter(params):
        (
            embed_matrix,
            embed_offset,
            sine_a,
            inner_matrix,
            inner_offset,
            sine_b,
            head_matrix,
            skip_gain,
        ) = params
        head_slice = lax.dynamic_slice_in_dim(head_matrix, chan_index * span_width, span_width, 1)
        rate_slice = lax.dynamic_slice_in_dim(decay_rate, chan_index * span_width, span_width, 0)
        skip_slice = lax.dynamic_slice_in_dim(skip_gain, chan_index * span_width, span_width, 0)
        impulse_part = filter_values(
            seq_length,
            embed_matrix,
            embed_offset,
            sine_a,
            inner_matrix,
            inner_offset,
            sine_b,
            head_slice,
            rate_slice,
        )
        return (impulse_part, skip_slice)

    filter_params = (
        embed_weight,
        embed_bias,
        first_sine,
        inner_weight,
        inner_bias,
        second_sine,
        filter_weight,
        long_bias,
    )
    (impulse, skip_part), filter_back = jax.vjp(local_filter, filter_params)
    skip_tiled = jnp.tile(skip_part, chan_count)
    forward_full, inverse_table = spectral_tables(block_rows)
    forward_half = forward_full[:, :block_rows]
    inverse_adjoint = inverse_table.T
    impulse_blocks = impulse.reshape(seq_count, block_rows, span_width)
    earlier = jnp.concatenate([jnp.zeros_like(impulse_blocks[:1]), impulse_blocks[:-1]], axis=0)
    segments = jnp.concatenate([earlier, impulse_blocks], axis=1)
    filt_spec = jnp.einsum("fm,nmc->nfc", forward_full, segments, precision=highest)
    filt_spec = filt_spec.reshape(seq_count, 2, freq_count, 1, span_width)
    zero_spec = jnp.zeros((2 * freq_count, width), jnp.float32)

    def contribution(spectrum, source):
        distance = seq_index - source
        causal = (distance >= 0).astype(jnp.float32)
        slot_index = jnp.clip(distance, 0, seq_count - 1)
        filt = lax.dynamic_index_in_dim(filt_spec, slot_index, 0, keepdims=False)
        shaped = spectrum.reshape(2, freq_count, chan_count, span_width)
        return causal * spec_product(filt, shaped).reshape(2 * freq_count, width)

    def micro_step(carry, inputs):
        grads, filt_grad, skip_grad = carry
        block_in, block_cot = inputs
        resid = block_in.astype(jnp.float32)
        normed_one, norm_back_one = jax.vjp(layer_norm, resid, gain_one_f, shift_one_f)
        normed_low = normed_one.astype(jnp.bfloat16)
        mixed = (
            jnp.dot(normed_low, mix_matrix, preferred_element_type=jnp.float32) + mix_offset_f
        ).astype(jnp.bfloat16)
        before = from_behind(mixed[block_rows - 2 :], "seq", 1)
        padded = jnp.concatenate([before, mixed], axis=0).astype(jnp.float32)
        short_out = (
            taps_f[0] * padded[:-2]
            + taps_f[1] * padded[1:-1]
            + taps_f[2] * padded[2:]
            + short_offset_f
        )
        gate_out = short_out[:, :width]
        gate_in = short_out[:, width : 2 * width]
        values = short_out[:, 2 * width :]
        product = (gate_in * values).astype(jnp.bfloat16)
        channel_view = lax.all_to_all(
            product.reshape(block_rows, chan_count, span_width),
            "ch",
            split_axis=1,
            concat_axis=1,
            tiled=True,
        ).reshape(block_rows, width)
        own_float = channel_view.astype(jnp.float32)
        own_spec = matmul(forward_half, own_float)
        shard_piece = lax.all_gather(channel_view[None], "seq", axis=0, tiled=True)

        def add_single(offset, partial_value):
            spectrum = matmul(forward_half, shard_piece[offset].astype(jnp.float32))
            return partial_value + contribution(spectrum, offset)

        summed = lax.fori_loop(0, shard_piece.shape[0], add_single, zero_spec)
        long_out = matmul(inverse_table, summed) + skip_tiled * own_float
        long_low = long_out.astype(jnp.bfloat16)
        token_view = lax.all_to_all(
            long_low.reshape(block_rows, chan_count, span_width),
            "ch",
            split_axis=1,
            concat_axis=1,
            tiled=True,
        ).reshape(block_rows, width)
        token_float = token_view.astype(jnp.float32)
        gated_out = (gate_out * token_float).astype(jnp.bfloat16)
        middle = (
            resid
            + jnp.dot(gated_out, out_matrix, preferred_element_type=jnp.float32)
            + out_offset_f
        )
        normed_two, norm_back_two = jax.vjp(layer_norm, middle, gain_two_f, shift_two_f)
        normed_two_low = normed_two.astype(jnp.bfloat16)
        hidden_pre = (
            jnp.dot(normed_two_low, expand_matrix, preferred_element_type=jnp.float32)
            + expand_offset_f
        )
        hidden_act, gelu_back = jax.vjp(exact_gelu, hidden_pre)
        hidden_low = hidden_act.astype(jnp.bfloat16)
        result = (
            middle
            + jnp.dot(hidden_low, shrink_matrix, preferred_element_type=jnp.float32)
            + shrink_offset_f
        )
        block_result = result.astype(jnp.bfloat16)
        grad_out = block_cot.astype(jnp.float32)
        shrink_grad = contract_rows(hidden_low, block_cot)
        shrink_off_grad = jnp.sum(grad_out, axis=0)
        hidden_grad = contract_cols(block_cot, shrink_matrix)
        pre_grad = gelu_back(hidden_grad)[0].astype(jnp.bfloat16)
        expand_grad = contract_rows(normed_two_low, pre_grad)
        expand_off_grad = jnp.sum(pre_grad.astype(jnp.float32), axis=0)
        normed_two_grad = contract_cols(pre_grad, expand_matrix)
        middle_ln_grad, gain_two_grad, shift_two_grad = norm_back_two(normed_two_grad)
        middle_grad = grad_out + middle_ln_grad
        branch_low = middle_grad.astype(jnp.bfloat16)
        out_grad = contract_rows(gated_out, branch_low)
        out_off_grad = jnp.sum(branch_low.astype(jnp.float32), axis=0)
        gated_grad = contract_cols(branch_low, out_matrix)
        gate_out_grad = gated_grad * token_float
        token_grad = (gated_grad * gate_out).astype(jnp.bfloat16)
        channel_grad = lax.all_to_all(
            token_grad.reshape(block_rows, chan_count, span_width),
            "ch",
            split_axis=1,
            concat_axis=1,
            tiled=True,
        ).reshape(block_rows, width)
        channel_grad_f = channel_grad.astype(jnp.float32)
        own_shaped = own_spec.reshape(2, freq_count, chan_count, span_width)

        def back_term(running, grad_spec, target):
            spec_acc, filt_acc = running
            distance = target - seq_index
            causal = (distance >= 0).astype(jnp.float32)
            slot_index = jnp.clip(distance, 0, seq_count - 1)
            filt = lax.dynamic_index_in_dim(filt_spec, slot_index, 0, keepdims=False)
            shaped = grad_spec.reshape(2, freq_count, chan_count, span_width)
            spec_acc = spec_acc + causal * spec_adjoint(filt, shaped).reshape(2 * freq_count, width)
            filt_term = causal * jnp.sum(spec_adjoint(own_shaped, shaped), axis=2, keepdims=True)
            current = lax.dynamic_index_in_dim(filt_acc, slot_index, 0, keepdims=True)
            filt_acc = lax.dynamic_update_index_in_dim(
                filt_acc, current + filt_term[None], slot_index, 0
            )
            return (spec_acc, filt_acc)

        back_shard_piece = lax.all_gather(channel_grad[None], "seq", axis=0, tiled=True)

        def back_single(offset, partial_value):
            grad_spec = matmul(inverse_adjoint, back_shard_piece[offset].astype(jnp.float32))
            return back_term(partial_value, grad_spec, offset)

        spec_grad, filt_grad = lax.fori_loop(
            0, back_shard_piece.shape[0], back_single, (zero_spec, filt_grad)
        )
        input_grad = (
            lax.dot_general(
                forward_half,
                spec_grad,
                (((0,), (0,)), ((), ())),
                precision=highest,
                preferred_element_type=jnp.float32,
            )
            + skip_tiled * channel_grad_f
        )
        skip_grad = skip_grad + jnp.sum(
            (channel_grad_f * own_float).reshape(block_rows, chan_count, span_width), axis=(0, 1)
        )
        input_low = input_grad.astype(jnp.bfloat16)
        token_input = (
            lax.all_to_all(
                input_low.reshape(block_rows, chan_count, span_width),
                "ch",
                split_axis=1,
                concat_axis=1,
                tiled=True,
            )
            .reshape(block_rows, width)
            .astype(jnp.float32)
        )
        short_grad = jnp.concatenate(
            [gate_out_grad, token_input * values, token_input * gate_in], axis=1
        )
        short_off_grad = jnp.sum(short_grad, axis=0)
        taps_grad = jnp.stack(
            [
                jnp.sum(short_grad * padded[:-2], axis=0),
                jnp.sum(short_grad * padded[1:-1], axis=0),
                jnp.sum(short_grad * padded[2:], axis=0),
            ]
        )
        padded_grad = (
            jnp.pad(taps_f[0] * short_grad, ((0, 2), (0, 0)))
            + jnp.pad(taps_f[1] * short_grad, ((1, 1), (0, 0)))
            + jnp.pad(taps_f[2] * short_grad, ((2, 0), (0, 0)))
        )
        after = from_behind(padded_grad[:2], "seq", -1)
        mixed_grad = padded_grad[2:] + jnp.concatenate(
            [jnp.zeros((block_rows - 2, 3 * width), jnp.float32), after], axis=0
        )
        mixed_low = mixed_grad.astype(jnp.bfloat16)
        mix_grad = contract_rows(normed_low, mixed_low)
        mix_off_grad = jnp.sum(mixed_low.astype(jnp.float32), axis=0)
        normed_one_grad = contract_cols(mixed_low, mix_matrix)
        resid_ln_grad, gain_one_grad, shift_one_grad = norm_back_one(normed_one_grad)
        tokens_grad = (middle_grad + resid_ln_grad).astype(jnp.bfloat16)
        step_grads = (
            gain_one_grad,
            shift_one_grad,
            mix_grad,
            mix_off_grad,
            taps_grad,
            short_off_grad,
            out_grad,
            out_off_grad,
            gain_two_grad,
            shift_two_grad,
            expand_grad,
            expand_off_grad,
            shrink_grad,
            shrink_off_grad,
        )
        grads = jax.tree.map(lambda left, right: left + right, grads, step_grads)
        return ((grads, filt_grad, skip_grad), (block_result, tokens_grad))

    zero_grads = tuple((jnp.zeros(item.shape, jnp.float32) for item in gathered))
    init = (zero_grads, jnp.zeros_like(filt_spec), jnp.zeros((span_width,), jnp.float32))
    (grads, filt_grad, skip_grad), (results, token_grads) = lax.scan(
        micro_step, init, (tokens[:, 0], cotangent[:, 0])
    )
    shards = (
        lax.psum_scatter(grads[0], ("ch", "seq"), scatter_dimension=0, tiled=True),
        lax.psum_scatter(grads[1], ("ch", "seq"), scatter_dimension=0, tiled=True),
        lax.psum_scatter(grads[2], ("ch", "seq"), scatter_dimension=0, tiled=True),
        lax.psum_scatter(grads[3], ("ch", "seq"), scatter_dimension=0, tiled=True),
        lax.psum_scatter(grads[4], ("ch", "seq"), scatter_dimension=1, tiled=True),
        lax.psum_scatter(grads[5], ("ch", "seq"), scatter_dimension=0, tiled=True),
        lax.psum_scatter(grads[6], ("ch", "seq"), scatter_dimension=0, tiled=True),
        lax.psum_scatter(grads[7], ("ch", "seq"), scatter_dimension=0, tiled=True),
        lax.psum_scatter(grads[8], ("ch", "seq"), scatter_dimension=0, tiled=True),
        lax.psum_scatter(grads[9], ("ch", "seq"), scatter_dimension=0, tiled=True),
        lax.psum_scatter(grads[10], ("ch", "seq"), scatter_dimension=0, tiled=True),
        lax.psum_scatter(grads[11], ("ch", "seq"), scatter_dimension=0, tiled=True),
        lax.psum_scatter(grads[12], ("ch", "seq"), scatter_dimension=0, tiled=True),
        lax.psum_scatter(grads[13], ("ch", "seq"), scatter_dimension=0, tiled=True),
    )
    segment_grad = jnp.einsum(
        "fm,nfc->nmc",
        forward_full,
        filt_grad.reshape(seq_count, 2 * freq_count, span_width),
        precision=highest,
    )
    impulse_grad = segment_grad[:, block_rows:] + jnp.concatenate(
        [segment_grad[1:, :block_rows], jnp.zeros((1, block_rows, span_width), jnp.float32)], axis=0
    )
    local_grads = filter_back((impulse_grad.reshape(seq_length, span_width), skip_grad))[0]
    summed_filter = lax.psum(local_grads, ("ch", "seq"))
    return (
        results[:, None],
        token_grads[:, None],
        shards[0],
        shards[1],
        shards[2],
        shards[3],
        shards[4],
        shards[5],
        summed_filter[0],
        summed_filter[1],
        summed_filter[2],
        summed_filter[3],
        summed_filter[4],
        summed_filter[5],
        summed_filter[6],
        summed_filter[7],
        shards[6],
        shards[7],
        shards[8],
        shards[9],
        shards[10],
        shards[11],
        shards[12],
        shards[13],
    )


def block(*args):
    tokens, expand_weight = args[0], args[21]
    n = Sizes(
        lax.axis_size("ch"), lax.axis_size("seq"), tokens.shape[2], tokens.shape[3], expand_weight.shape[1]
    )
    if n.own % 8 == 0 and n.pair % 16 == 0 and n.unit % 16 == 0 and n.block == LANES:
        return fused(n, *args)
    return on_device(*args)


def solution(mesh):
    return jax.shard_map(
        block,
        mesh=mesh,
        in_specs=(
            P(None, "ch", "seq", None),
            P(None, "ch", "seq", None),
            P(("ch", "seq")),
            P(("ch", "seq")),
            P(("ch", "seq"), None),
            P(("ch", "seq")),
            P(None, ("ch", "seq")),
            P(("ch", "seq")),
            P(),
            P(),
            P(),
            P(),
            P(),
            P(),
            P(),
            P(),
            P(),
            P(("ch", "seq"), None),
            P(("ch", "seq")),
            P(("ch", "seq")),
            P(("ch", "seq")),
            P(("ch", "seq"), None),
            P(("ch", "seq")),
            P(("ch", "seq"), None),
            P(("ch", "seq")),
        ),
        out_specs=(
            P(None, "ch", "seq", None),
            P(None, "ch", "seq", None),
            P(("ch", "seq")),
            P(("ch", "seq")),
            P(("ch", "seq"), None),
            P(("ch", "seq")),
            P(None, ("ch", "seq")),
            P(("ch", "seq")),
            P(),
            P(),
            P(),
            P(),
            P(),
            P(),
            P(),
            P(),
            P(("ch", "seq"), None),
            P(("ch", "seq")),
            P(("ch", "seq")),
            P(("ch", "seq")),
            P(("ch", "seq"), None),
            P(("ch", "seq")),
            P(("ch", "seq"), None),
            P(("ch", "seq")),
        ),
        check_vma=False,
    )
```

profile of v0, /device:TPU:1, one launch (start us, length us, event | category | flops | bytes accessed | tf_op | source)
XLA Modules:
  0.0 194.8 jit_solution(15129707080660872717)
XLA Ops:
  0.7 190.9 %shard_map.442 = (bf16[2,128,768]{2,1,0:T(8,128)(2,1)}, bf16[2,128,768]{2,1,0:T(8,128)(2,1)}, f32[2,24,1152]{2,1,0:T(8,128)}, f32[2,24,1536]{2,1,0:T(8,128)}, f3...) custom-call(bf16[2,1,128,768]{3,2,1,0:T(8,128)(2,1)} %refs_0_.1, ...), custom_call_target="tpu_custom_call" | custom-call | tf_op jit(solution)/shard_map/pallas_call | solution.py:1249
  191.6 3.0 %shard_map.443 = (bf16[2,1,128,768]{3,2,1,0:T(8,128)(2,1)}, bf16[2,1,128,768]{3,2,1,0:T(8,128)(2,1)}, f32[24]{0:T(128)}, f32[24]{0:T(128)}, f32[24,2304]{1,0:T(8...) custom-call(bf16[2,128,768]{2,1,0:T(8,128)(2,1)} %get-tuple-element., ...), custom_call_target="tpu_custom_call" | custom-call | tf_op jit(solution)/shard_map/pallas_call | solution.py:1261
where the time goes:
time: 195 us
  Pallas kernels  194 us (99%)
    pallas_call x1, Pallas kernels, fused(): pl.pallas_call(functools.partial(fused_kernel, n, names), out_shape=outs,...  191 us

commit v1 on v0

--- a/solution.py
+++ b/solution.py
@@ -701,7 +701,7 @@
 
     wait_u = to_channels(0, lambda s: gate(s, 1) * gate(s, 2))
     third = n.own // 3
-    pump(14)
+    pump(14 + 16 + 2)
     filter_setup()
     filter_first()
     filter_second()
@@ -711,7 +711,7 @@
     vectors_from_shards(*groups[2])
     for q in range(3):
         lax.fori_loop(q * third, (q + 1) * third, lambda r, carry: (toeplitz(r), carry)[1], 0)
-    pump(12)
+    pump(10)
     wait_u()
 
     group = n.y_n * 4

time: 195 us -> 193 us (0.990)
  Pallas kernels: 194 us -> 192 us
where the time goes in v1:
time: 193 us
  Pallas kernels  192 us (99%)
    pallas_call x1, Pallas kernels, fused(): pl.pallas_call(functools.partial(fused_kernel, n, names), out_shape=outs,...  189 us

profile of v1, /device:TPU:1, one launch (start us, length us, event | category | flops | bytes accessed | tf_op | source)
XLA Modules:
  0.0 193.0 jit_solution(18412889425016748710)
XLA Ops:
  0.7 189.1 %shard_map.442 = (bf16[2,128,768]{2,1,0:T(8,128)(2,1)}, bf16[2,128,768]{2,1,0:T(8,128)(2,1)}, f32[2,24,1152]{2,1,0:T(8,128)}, f32[2,24,1536]{2,1,0:T(8,128)}, f3...) custom-call(bf16[2,1,128,768]{3,2,1,0:T(8,128)(2,1)} %refs_0_.1, ...), custom_call_target="tpu_custom_call" | custom-call | tf_op jit(solution)/shard_map/pallas_call | solution.py:1249
  189.8 3.0 %shard_map.443 = (bf16[2,1,128,768]{3,2,1,0:T(8,128)(2,1)}, bf16[2,1,128,768]{3,2,1,0:T(8,128)(2,1)}, f32[24]{0:T(128)}, f32[24]{0:T(128)}, f32[24,2304]{1,0:T(8...) custom-call(bf16[2,128,768]{2,1,0:T(8,128)(2,1)} %get-tuple-element., ...), custom_call_target="tpu_custom_call" | custom-call | tf_op jit(solution)/shard_map/pallas_call | solution.py:1261
